TPU v7x, 256 devices: a whole 4x4x8 slice. The times are simulated.
256 devices in a mesh: blk: 8 (over y, x_hi), dom: 32 (over z, x_lo, core).
Axes of the slice: x: 4 (x_hi: 2, x_lo: 2; x = x_hi * 2 + x_lo), y: 4, z: 8, core: 2. Of those that a mesh axis runs over, the one named last changes fastest.
Arguments:
- cell_features: bfloat16 [32, 2048, 768], P('dom', 'blk'), may hold values from -6 to 6
- cotangent: bfloat16 [32, 2048, 768], P('dom', 'blk'), may hold values from -6 to 6
- query_weight: bfloat16 [768, 768], replicated
- key_weight: bfloat16 [768, 768], replicated
- value_weight: bfloat16 [768, 768], replicated, may hold values from -0.21875 to 0.21875
- out_weight: bfloat16 [768, 768], replicated, may hold values from -0.21875 to 0.21875
- anchor_index: int32 [32, 256], P('dom', 'blk'), may hold values from 0 to 255, as said below
- face_cells: int32 [32, 8, 2, 128], P('dom', 'blk'), may hold values from 0 to 255, as said below
- halo_count: int32 [32, 8, 2], P('dom', 'blk'), may hold values from 0 to 128, as said below
- neighbour_blocks: int32 [32, 16, 3], P('dom', 'blk'), may hold values from 0 to 3, as said below
Outputs:
- mixed: bfloat16 [32, 2048, 768], P('dom', 'blk')
- cell_grad: bfloat16 [32, 2048, 768], P('dom', 'blk')
- weight_grads: float32 [3072, 768], P(('blk', 'dom'))
Inputs may be any that keep to these rules, and one draw needn't show every extreme that they name: `anchor_index`: the 32 entries of one slot are different cells of that slot. `face_cells`: the 256 entries of one slot are different cells of that slot. halo_count[0, b, 0] and halo_count[31, b, 1] are 0 for every b; all other entries are 1 or more. `neighbour_blocks`: row b*2+j lists 3 different pool blocks, the first of them j itself.
All inputs are finite; a program needn't handle non-finite values.
Results may differ from a plain program's by a relative error of at most 0.017.
The roundings to bfloat16 on the way count: a program that leaves them out, or rounds other values in their place, can miss the bound.
Values may be sent and summed in bfloat16 or wider, within the bound.
No kernel may reach another device: no remote copies, remote signals or barrier semaphores. Data moves between devices by JAX's collectives and lax.ppermute only.
A program may use at most 128 MiB of HBM per device.

v0:
```python
import math

import jax
import jax.numpy as jnp
from jax import lax
from jax.sharding import PartitionSpec as P

HEADS = 12
BS = 128
NB = 3


EPSILON = 1e-06
MASKED = -1e30


def extended_2(block, sides, width):
    for axis, dim in sides:
        count = lax.axis_size(axis)
        forward = [(i, i + 1) for i in range(count - 1)]
        backward = [(target, source) for source, target in forward]
        low = lax.ppermute(
            lax.slice_in_dim(block, block.shape[dim] - width, None, axis=dim), axis, forward
        )
        high = lax.ppermute(lax.slice_in_dim(block, 0, width, axis=dim), axis, backward)
        block = jnp.concatenate([low, block, high], axis=dim)
    return block


def split_heads(tensor):
    leading = tensor.shape[:-2]
    length = tensor.shape[-2]
    tensor = tensor.reshape(leading + (length, HEADS, tensor.shape[-1] // HEADS))
    return jnp.moveaxis(tensor, -2, -3)


def join_heads(tensor):
    tensor = jnp.moveaxis(tensor, -3, -2)
    return tensor.reshape(tensor.shape[:-2] + (tensor.shape[-2] * tensor.shape[-1],))


def attend(queries, key_rows, value_rows, upstream, validity):
    scaling = 1.0 / math.sqrt(queries.shape[-1])
    scores = (
        jnp.einsum("...qe,...ke->...qk", queries, key_rows, preferred_element_type=jnp.float32)
        * scaling
    )
    scores = jnp.where(validity[..., None, :], scores, MASKED)
    highest = jnp.max(scores, axis=-1, keepdims=True)
    powers = jnp.exp(scores - highest)
    probability = powers / jnp.sum(powers, axis=-1, keepdims=True)
    prob_rounded = probability.astype(jnp.bfloat16)
    out_rows = jnp.einsum(
        "...qk,...ke->...qe", prob_rounded, value_rows, preferred_element_type=jnp.float32
    )
    prob_grad = jnp.einsum(
        "...qe,...ke->...qk", upstream, value_rows, preferred_element_type=jnp.float32
    )
    score_grad = probability * (
        prob_grad - jnp.sum(probability * prob_grad, axis=-1, keepdims=True)
    )
    score_rounded = score_grad.astype(jnp.bfloat16)
    query_term = (
        jnp.einsum(
            "...qk,...ke->...qe", score_rounded, key_rows, preferred_element_type=jnp.float32
        )
        * scaling
    )
    key_term = (
        jnp.einsum("...qk,...qe->...ke", score_rounded, queries, preferred_element_type=jnp.float32)
        * scaling
    )
    value_term = jnp.einsum(
        "...qk,...qe->...ke", prob_rounded, upstream, preferred_element_type=jnp.float32
    )
    return (out_rows, query_term, key_term, value_term)


def body(
    cell_features,
    cotangent,
    query_weight,
    key_weight,
    value_weight,
    out_weight,
    anchor_index,
    face_cells,
    halo_count,
    neighbour_blocks,
):
    x_local = cell_features[0]
    dy_local = cotangent[0]
    cell_count, width = x_local.shape
    block_count = cell_count // BS
    as_float = x_local.astype(jnp.float32)
    inverse = lax.rsqrt(jnp.mean(as_float * as_float, axis=-1, keepdims=True) + EPSILON)
    normed = (as_float * inverse).astype(jnp.bfloat16)
    w_merged = jnp.concatenate([query_weight, key_weight, value_weight], axis=1)
    projected = jnp.dot(normed, w_merged, preferred_element_type=jnp.float32).astype(jnp.bfloat16)
    queries = projected[:, :width]
    keyval_local = projected[:, width:]
    grad_mid = jnp.dot(dy_local, out_weight.T, preferred_element_type=jnp.float32).astype(
        jnp.bfloat16
    )
    anchor_rows = anchor_index[0]
    anchors = lax.all_gather(keyval_local[anchor_rows], "blk", axis=0, tiled=True)
    face_rows = face_cells[0, 0].reshape(2 * BS)
    live_count = halo_count[0, 0]
    extended = extended_2(keyval_local[face_rows], (("dom", 0),), BS)
    halo_keyval = jnp.concatenate([extended[:BS], extended[3 * BS :]], 0)
    key_pool = jnp.concatenate([keyval_local, halo_keyval], 0).reshape(
        block_count + 2, BS, 2 * width
    )
    positions = jnp.arange(BS)
    live_rows = jnp.concatenate(
        [
            jnp.ones((block_count, BS), bool),
            (positions < live_count[0])[None],
            (positions < live_count[1])[None],
        ],
        0,
    )
    near_index = neighbour_blocks[0]
    chosen = key_pool[near_index].reshape(block_count, NB * BS, 2 * width)
    chosen_live = live_rows[near_index].reshape(block_count, 1, NB * BS)
    all_live = jnp.ones((anchors.shape[0],), bool)

    def head_pass(members):
        return attend(members[0], members[1], members[2], members[3], all_live)

    anchor_out, anchor_dquery, anchor_dkey, anchor_dvalue = lax.map(
        head_pass,
        (
            split_heads(queries),
            split_heads(anchors[:, :width]),
            split_heads(anchors[:, width:]),
            split_heads(grad_mid),
        ),
    )
    near_out, near_dquery, near_dkey, near_dvalue = attend(
        split_heads(queries.reshape(block_count, BS, width)),
        split_heads(chosen[..., :width]),
        split_heads(chosen[..., width:]),
        split_heads(grad_mid.reshape(block_count, BS, width)),
        chosen_live,
    )
    attended = (join_heads(anchor_out) + join_heads(near_out).reshape(cell_count, width)).astype(
        jnp.bfloat16
    )
    query_grad = (
        join_heads(anchor_dquery) + join_heads(near_dquery).reshape(cell_count, width)
    ).astype(jnp.bfloat16)
    chosen_grad = jnp.concatenate([join_heads(near_dkey), join_heads(near_dvalue)], -1)
    chosen_grad = chosen_grad.reshape(block_count * NB, BS, 2 * width)
    onehot = (near_index.reshape(-1)[:, None] == jnp.arange(block_count + 2)[None, :]).astype(
        jnp.float32
    )
    pool_grad = jnp.einsum("sp,sbf->pbf", onehot, chosen_grad, precision=lax.Precision.HIGHEST)
    anchor_term = jnp.concatenate([join_heads(anchor_dkey), join_heads(anchor_dvalue)], -1)
    anchor_term = lax.optimization_barrier(anchor_term.astype(jnp.bfloat16)).astype(jnp.float32)
    anchor_share = lax.psum_scatter(
        anchor_term.astype(jnp.bfloat16), "blk", scatter_dimension=0, tiled=True
    ).astype(jnp.float32)
    halo_grad = pool_grad[block_count:].reshape(2 * BS, 2 * width).astype(jnp.bfloat16)
    returned = extended_2(halo_grad, (("dom", 0),), BS)
    came_back = jnp.concatenate([returned[:BS], returned[3 * BS :]], 0).astype(jnp.float32)
    keyval_grad = pool_grad[:block_count].reshape(cell_count, 2 * width)
    keyval_grad = keyval_grad.at[jnp.concatenate([anchor_rows, face_rows])].add(
        jnp.concatenate([anchor_share, came_back], 0)
    )
    proj_grads = jnp.concatenate([query_grad, keyval_grad.astype(jnp.bfloat16)], 1)
    inner_term = jnp.dot(normed.T, proj_grads, preferred_element_type=jnp.float32)
    inner_term = inner_term.reshape(width, 3, width).transpose(1, 0, 2).reshape(3 * width, width)
    out_term = jnp.dot(attended.T, dy_local, preferred_element_type=jnp.float32)
    weight_term = jnp.concatenate([inner_term, out_term], 0)
    weight_grads = lax.psum_scatter(weight_term, ("blk", "dom"), scatter_dimension=0, tiled=True)
    normed_grad = jnp.dot(proj_grads, w_merged.T, preferred_element_type=jnp.float32)
    cot_float = dy_local.astype(jnp.float32)
    cube = inverse * inverse * inverse
    cell_grad = (
        cot_float
        + inverse * normed_grad
        - as_float * cube * jnp.mean(normed_grad * as_float, axis=-1, keepdims=True)
    )
    mixed = as_float + jnp.dot(attended, out_weight, preferred_element_type=jnp.float32)
    return (mixed.astype(jnp.bfloat16)[None], cell_grad.astype(jnp.bfloat16)[None], weight_grads)


def solution(mesh):
    return jax.shard_map(
        body,
        mesh=mesh,
        in_specs=(
            P("dom", "blk", None),
            P("dom", "blk", None),
            P(),
            P(),
            P(),
            P(),
            P("dom", "blk"),
            P("dom", "blk", None, None),
            P("dom", "blk", None),
            P("dom", "blk", None),
        ),
        out_specs=(P("dom", "blk", None), P("dom", "blk", None), P(("blk", "dom"), None)),
        check_vma=False,
    )
```

profile of v0, /device:TPU:24, one launch (start us, length us, event | category | flops | bytes accessed | tf_op | source)
XLA Modules:
  0.0 1583.1 jit_solution(9789247600254076824)
XLA Ops:
  22.3 37.7 %all-gather = bf16[256,1536]{1,0:T(8,128)(2,1)S(1)} all-gather(bf16[32,1536]{1,0:T(8,128)(2,1)} %gather_fusion), channel_id=2, replica_groups=mesh['blk'=8,'dom'=32] {'blk'}, dimensions={0}, use_global_device_ids=true | all-gather | bytes 884736 | tf_op jit(solution)/shard_map/all_gather | solution.py:106
  67.2 75.0 %while.16 = (s32[]{:T(128)}, f32[12,256,64]{1,2,0:T(8,128)S(1)}, f32[12,256,64]{1,2,0:T(8,128)}, bf16[12,256,64]{1,2,0:T(8,128)(2,1)}, bf16[12,256,64]{1,2,0:T(8...) while((s32[]{:T(128)}, f32[12,256,64]{1,2,0:T(8,128)S(1)}, ...), condition=%wide.region_5.6_spmd, body=%wide.region_1.5_spmd.sunk | while | flops 51608832 | bytes 3034221 | solution.py:131
  252.8 634.7 %fusion = f32[16,768]{1,0:T(8,128)S(1)} fusion(f32[3072,768]{1,0:T(8,128)} %pad_maximum_fusion), kind=kCustom, calls=%all-reduce-scatter | all-reduce-scatter fusion | flops 3145729 | bytes 9486336
  887.5 77.5 %collective-permute-start.66 = (f32[16,768]{1,0:T(8,128)S(1)}, f32[16,768]{1,0:T(8,128)S(1)}, u32[]{:S(2)}, u32[]{:S(2)}) collective-permute-start(f32[16,768]{1,0:T(8,128)S(1)} %fusion), channel_id=1, source_target_pairs={{0,63},{1,64},{2,65},{3,66},{4,67},{5,68},{6,69},{7,70},{8,71},{9,... | collective-permute-start | bytes 147464
  1048.9 24.0 %collective-permute-start.34 = (f32[16,768]{1,0:T(8,128)S(1)}, f32[16,768]{1,0:T(8,128)S(1)}, u32[]{:S(2)}, u32[]{:S(2)}) collective-permute-start(f32[16,768]{1,0:T(8,128)S(1)} %fusion), channel_id=1, source_target_pairs={{0,31},{1,32},{2,33},{3,34},{4,35},{5,36},{6,37},{7,38},{8,39},{9,... | collective-permute-start | bytes 147464
  1072.9 13.1 collective-permute-start.33
  1086.0 13.1 collective-permute-start.32
  1099.2 13.1 collective-permute-start.31
  1112.3 13.1 collective-permute-start.30
  1125.5 13.1 collective-permute-start.29
  1139.6 13.3 collective-permute-start.28
  1152.8 13.1 collective-permute-start.27
  1166.0 13.1 collective-permute-start.26
  1179.1 13.1 collective-permute-start.25
  1192.3 13.1 collective-permute-start.24
  1205.5 13.1 collective-permute-start.23
  1218.7 13.1 collective-permute-start.22
  1231.8 13.1 collective-permute-start.21
  1245.0 13.1 collective-permute-start.20
  1258.1 13.1 collective-permute-start.19
  1272.8 13.3 collective-permute-start.18
  1286.1 13.1 collective-permute-start.17
  1458.9 13.3 collective-permute-start.4
  1480.8 93.8 %concatenate.69 = f32[1036,768]{1,0:T(8,128)} concatenate(f32[12,768]{1,0:T(8,128)S(1)} %collective-permute-done.67, f32[16,768]{1,0:T(8,128)S(1)} %collective-permute-done.66, f32[16,768]{1,0:T(8,128)S(1)} %collective-permute-done.65, f32[16,768]{1,0:T(8,128)S(1)} %collective-permute-done.64, f32[16,768]{1,0:T(8,128)S(1)} %collective-permute-done.63, ...), dimensions={0} | concatenate | bytes 6365184
  (516 shorter events, 461.8 us)
Async XLA Ops:
  7.2 219.9 %reduce-scatter.6.cloned.1.call-start = ((), (), s32[]{:S(2)}) async-start(), calls=%async_computation.1 | async-start | bytes 884736 | tf_op jit(solution)/shard_map/reduce_scatter | solution.py:161
  14.7 140.8 %collective-permute-start.1 = (bf16[128,1536]{1,0:T(8,128)(2,1)}, bf16[128,1536]{1,0:T(8,128)(2,1)}, u32[]{:S(2)}, u32[]{:S(2)}) collective-permute-start(bf16[128,1536]{1,0:T(8,128)(2,1)} %get-tuple-element.113), channel_id=1, source_target_pairs={{1,0},{2,1},{3,2},{4,3},{5,4},{6,5},{7,6},{8,7},{9,8},{10,9},{11,1... | collective-permute-start | bytes 1179656 | tf_op jit(solution)/shard_map/ppermute | solution.py:25
  16.0 139.5 %collective-permute-start = (bf16[128,1536]{1,0:T(8,128)(2,1)}, bf16[128,1536]{1,0:T(8,128)(2,1)}, u32[]{:S(2)}, u32[]{:S(2)}) collective-permute-start(bf16[128,1536]{1,0:T(8,128)(2,1)} %get-tuple-element.112), channel_id=1, source_target_pairs={{0,1},{1,2},{2,3},{3,4},{4,5},{5,6},{6,7},{7,8},{8,9},{9,10},{10,1... | collective-permute-start | bytes 1179656 | tf_op jit(solution)/shard_map/ppermute | solution.py:22
  887.5 89.3 %collective-permute-start.66 = (f32[16,768]{1,0:T(8,128)S(1)}, f32[16,768]{1,0:T(8,128)S(1)}, u32[]{:S(2)}, u32[]{:S(2)}) collective-permute-start(f32[16,768]{1,0:T(8,128)S(1)} %fusion), channel_id=1, source_target_pairs={{0,63},{1,64},{2,65},{3,66},{4,67},{5,68},{6,69},{7,70},{8,71},{9,... | collective-permute-start | bytes 147464
  1048.9 76.6 %collective-permute-start.34 = (f32[16,768]{1,0:T(8,128)S(1)}, f32[16,768]{1,0:T(8,128)S(1)}, u32[]{:S(2)}, u32[]{:S(2)}) collective-permute-start(f32[16,768]{1,0:T(8,128)S(1)} %fusion), channel_id=1, source_target_pairs={{0,31},{1,32},{2,33},{3,34},{4,35},{5,36},{6,37},{7,38},{8,39},{9,... | collective-permute-start | bytes 147464
  1072.9 66.7 %collective-permute-start.33 = (f32[16,768]{1,0:T(8,128)S(1)}, f32[16,768]{1,0:T(8,128)}, u32[]{:S(2)}, u32[]{:S(2)}) collective-permute-start(f32[16,768]{1,0:T(8,128)S(1)} %fusion), channel_id=1, source_target_pairs={{0,30},{1,31},{2,32},{3,33},{4,34},{5,35},{6,36},{7,37},{8,38},{9,... | collective-permute-start | bytes 147464
  1086.0 66.8 %collective-permute-start.32 = (f32[16,768]{1,0:T(8,128)S(1)}, f32[16,768]{1,0:T(8,128)}, u32[]{:S(2)}, u32[]{:S(2)}) collective-permute-start(f32[16,768]{1,0:T(8,128)S(1)} %fusion), channel_id=1, source_target_pairs={{0,29},{1,30},{2,31},{3,32},{4,33},{5,34},{6,35},{7,36},{8,37},{9,... | collective-permute-start | bytes 147464
  1099.2 66.8 %collective-permute-start.31 = (f32[16,768]{1,0:T(8,128)S(1)}, f32[16,768]{1,0:T(8,128)}, u32[]{:S(2)}, u32[]{:S(2)}) collective-permute-start(f32[16,768]{1,0:T(8,128)S(1)} %fusion), channel_id=1, source_target_pairs={{0,28},{1,29},{2,30},{3,31},{4,32},{5,33},{6,34},{7,35},{8,36},{9,... | collective-permute-start | bytes 147464
  1112.3 66.8 %collective-permute-start.30 = (f32[16,768]{1,0:T(8,128)S(1)}, f32[16,768]{1,0:T(8,128)}, u32[]{:S(2)}, u32[]{:S(2)}) collective-permute-start(f32[16,768]{1,0:T(8,128)S(1)} %fusion), channel_id=1, source_target_pairs={{0,27},{1,28},{2,29},{3,30},{4,31},{5,32},{6,33},{7,34},{8,35},{9,... | collective-permute-start | bytes 147464
  1125.5 66.7 %collective-permute-start.29 = (f32[16,768]{1,0:T(8,128)S(1)}, f32[16,768]{1,0:T(8,128)}, u32[]{:S(2)}, u32[]{:S(2)}) collective-permute-start(f32[16,768]{1,0:T(8,128)S(1)} %fusion), channel_id=1, source_target_pairs={{0,26},{1,27},{2,28},{3,29},{4,30},{5,31},{6,32},{7,33},{8,34},{9,... | collective-permute-start | bytes 147464
  1139.6 66.0 %collective-permute-start.28 = (f32[16,768]{1,0:T(8,128)S(1)}, f32[16,768]{1,0:T(8,128)S(1)}, u32[]{:S(2)}, u32[]{:S(2)}) collective-permute-start(f32[16,768]{1,0:T(8,128)S(1)} %fusion), channel_id=1, source_target_pairs={{0,25},{1,26},{2,27},{3,28},{4,29},{5,30},{6,31},{7,32},{8,33},{9,... | collective-permute-start | bytes 147464
  1179.1 65.8 %collective-permute-start.25 = (f32[16,768]{1,0:T(8,128)S(1)}, f32[16,768]{1,0:T(8,128)S(1)}, u32[]{:S(2)}, u32[]{:S(2)}) collective-permute-start(f32[16,768]{1,0:T(8,128)S(1)} %fusion), channel_id=1, source_target_pairs={{0,22},{1,23},{2,24},{3,25},{4,26},{5,27},{6,28},{7,29},{8,30},{9,... | collective-permute-start | bytes 147464
  1192.3 65.9 %collective-permute-start.24 = (f32[16,768]{1,0:T(8,128)S(1)}, f32[16,768]{1,0:T(8,128)S(1)}, u32[]{:S(2)}, u32[]{:S(2)}) collective-permute-start(f32[16,768]{1,0:T(8,128)S(1)} %fusion), channel_id=1, source_target_pairs={{0,21},{1,22},{2,23},{3,24},{4,25},{5,26},{6,27},{7,28},{8,29},{9,... | collective-permute-start | bytes 147464
  1205.5 67.2 %collective-permute-start.23 = (f32[16,768]{1,0:T(8,128)S(1)}, f32[16,768]{1,0:T(8,128)S(1)}, u32[]{:S(2)}, u32[]{:S(2)}) collective-permute-start(f32[16,768]{1,0:T(8,128)S(1)} %fusion), channel_id=1, source_target_pairs={{0,20},{1,21},{2,22},{3,23},{4,24},{5,25},{6,26},{7,27},{8,28},{9,... | collective-permute-start | bytes 147464
  1218.7 67.4 %collective-permute-start.22 = (f32[16,768]{1,0:T(8,128)S(1)}, f32[16,768]{1,0:T(8,128)S(1)}, u32[]{:S(2)}, u32[]{:S(2)}) collective-permute-start(f32[16,768]{1,0:T(8,128)S(1)} %fusion), channel_id=1, source_target_pairs={{0,19},{1,20},{2,21},{3,22},{4,23},{5,24},{6,25},{7,26},{8,27},{9,... | collective-permute-start | bytes 147464
  1231.8 67.4 %collective-permute-start.21 = (f32[16,768]{1,0:T(8,128)S(1)}, f32[16,768]{1,0:T(8,128)S(1)}, u32[]{:S(2)}, u32[]{:S(2)}) collective-permute-start(f32[16,768]{1,0:T(8,128)S(1)} %fusion), channel_id=1, source_target_pairs={{0,18},{1,19},{2,20},{3,21},{4,22},{5,23},{6,24},{7,25},{8,26},{9,... | collective-permute-start | bytes 147464
  1245.0 67.4 %collective-permute-start.20 = (f32[16,768]{1,0:T(8,128)S(1)}, f32[16,768]{1,0:T(8,128)S(1)}, u32[]{:S(2)}, u32[]{:S(2)}) collective-permute-start(f32[16,768]{1,0:T(8,128)S(1)} %fusion), channel_id=1, source_target_pairs={{0,17},{1,18},{2,19},{3,20},{4,21},{5,22},{6,23},{7,24},{8,25},{9,... | collective-permute-start | bytes 147464
  1258.1 67.4 %collective-permute-start.19 = (f32[16,768]{1,0:T(8,128)S(1)}, f32[16,768]{1,0:T(8,128)S(1)}, u32[]{:S(2)}, u32[]{:S(2)}) collective-permute-start(f32[16,768]{1,0:T(8,128)S(1)} %fusion), channel_id=1, source_target_pairs={{0,16},{1,17},{2,18},{3,19},{4,20},{5,21},{6,22},{7,23},{8,24},{9,... | collective-permute-start | bytes 147464
  1272.8 67.8 %collective-permute-start.18 = (f32[16,768]{1,0:T(8,128)S(1)}, f32[16,768]{1,0:T(8,128)S(1)}, u32[]{:S(2)}, u32[]{:S(2)}) collective-permute-start(f32[16,768]{1,0:T(8,128)S(1)} %fusion), channel_id=1, source_target_pairs={{0,15},{1,16},{2,17},{3,18},{4,19},{5,20},{6,21},{7,22},{8,23},{9,... | collective-permute-start | bytes 147464
  1286.1 67.6 %collective-permute-start.17 = (f32[16,768]{1,0:T(8,128)S(1)}, f32[16,768]{1,0:T(8,128)S(1)}, u32[]{:S(2)}, u32[]{:S(2)}) collective-permute-start(f32[16,768]{1,0:T(8,128)S(1)} %fusion), channel_id=1, source_target_pairs={{0,14},{1,15},{2,16},{3,17},{4,18},{5,19},{6,20},{7,21},{8,22},{9,... | collective-permute-start | bytes 147464
  1299.2 67.6 %collective-permute-start.16 = (f32[16,768]{1,0:T(8,128)S(1)}, f32[16,768]{1,0:T(8,128)S(1)}, u32[]{:S(2)}, u32[]{:S(2)}) collective-permute-start(f32[16,768]{1,0:T(8,128)S(1)} %fusion), channel_id=1, source_target_pairs={{0,13},{1,14},{2,15},{3,16},{4,17},{5,18},{6,19},{7,20},{8,21},{9,... | collective-permute-start | bytes 147464
  1312.4 67.6 %collective-permute-start.15 = (f32[16,768]{1,0:T(8,128)S(1)}, f32[16,768]{1,0:T(8,128)S(1)}, u32[]{:S(2)}, u32[]{:S(2)}) collective-permute-start(f32[16,768]{1,0:T(8,128)S(1)} %fusion), channel_id=1, source_target_pairs={{0,12},{1,13},{2,14},{3,15},{4,16},{5,17},{6,18},{7,19},{8,20},{9,... | collective-permute-start | bytes 147464
  1326.2 67.0 %collective-permute-start.14 = (f32[16,768]{1,0:T(8,128)S(1)}, f32[16,768]{1,0:T(8,128)S(1)}, u32[]{:S(2)}, u32[]{:S(2)}) collective-permute-start(f32[16,768]{1,0:T(8,128)S(1)} %fusion), channel_id=1, source_target_pairs={{0,11},{1,12},{2,13},{3,14},{4,15},{5,16},{6,17},{7,18},{8,19},{9,... | collective-permute-start | bytes 147464
  1406.3 66.9 %collective-permute-start.8 = (f32[16,768]{1,0:T(8,128)S(1)}, f32[16,768]{1,0:T(8,128)S(1)}, u32[]{:S(2)}, u32[]{:S(2)}) collective-permute-start(f32[16,768]{1,0:T(8,128)S(1)} %fusion), channel_id=1, source_target_pairs={{0,5},{1,6},{2,7},{3,8},{4,9},{5,10},{6,11},{7,12},{8,13},{9,14},{... | collective-permute-start | bytes 147464
  (152 other events, 13525.5 us)
Sparse Core Ops, SparseCore 0:
  145.7 81.4 reduce-scatter.5
where the time goes:
time: 1600 us; the launch traced here: 1580 us
  blocking collectives  672 us (42%)
  starting transfers between devices  567 us (35%)
  local copies, waits for them, and re-layouts  158 us (10%)
  matrix products  104 us (6%)
  waiting for transfers between devices  35.4 us (2%)
  other arithmetic  29.8 us (2%)
  between operations  16.7 us (1%)
    unnamed x1, blocking collectives  635 us
    unnamed x64, starting transfers between devices  556 us
    unnamed x225, local copies, waits for them, and re-layouts  109 us
    all_gather x1, blocking collectives, body(): lax.all_gather(keyval_local[anchor_rows], 'blk', axis=0, tiled=True)  37.7 us
  transfers between devices with their start and end apart: 69, of which 13 were waited for; matrix products, arithmetic and copies ran while one was open for 10% of the time, Pallas kernels for 0%

commit v1 on v0

v1 whole, which is shorter than its diff:
```python
import jax
import jax.numpy as jnp
from jax import lax
from jax.experimental import pallas as pl
from jax.experimental.pallas import tpu as pltpu
from jax.sharding import Mesh, PartitionSpec as P

HEADS = 12
BS = 128
NB = 3
D = 768
CELLS = 256
ANCHORS = 256
POOL_ROWS = 512
KEY_ROWS = 768
HEAD = 64
SIDE = 384
PAIR = 128
SCALE = 0.125
EPSILON = 1e-06
MASKED = -1e30

f32 = jnp.float32
bf16 = jnp.bfloat16

NN = (((1,), (0,)), ((), ()))
NT = (((1,), (1,)), ((), ()))
TN = (((0,), (0,)), ((), ()))


def dot(a, b, dims=NN):
    return lax.dot_general(a, b, dims, preferred_element_type=f32)


def params(mib):
    return pltpu.CompilerParams(vmem_limit_bytes=mib << 20)


def send_kernel(x_ref, anchor_ref, face_ref, normed_ref, rows_a_ref, rows_lo_ref, rows_hi_ref):
    x = x_ref[...].astype(f32)
    inverse = lax.rsqrt(jnp.mean(x * x, axis=-1, keepdims=True) + EPSILON)
    normed = (x * inverse).astype(bf16)
    normed_ref[...] = normed

    def picked(index_row):
        cells = lax.broadcasted_iota(jnp.int32, (CELLS, index_row.shape[1]), 0)
        one_hot = (cells == index_row).astype(bf16)
        return dot(one_hot, normed, TN).astype(bf16)

    rows_a_ref[...] = picked(anchor_ref[...])
    rows_lo_ref[...] = picked(face_ref[0:1, :])
    rows_hi_ref[...] = picked(face_ref[1:2, :])


def send_call(x, anchor_row, face_rows):
    shapes = [(CELLS, D), (32, D), (BS, D), (BS, D)]
    return pl.pallas_call(
        send_kernel,
        out_shape=[jax.ShapeDtypeStruct(s, bf16) for s in shapes],
        compiler_params=params(32),
    )(x, anchor_row, face_rows)


def project_kernel(n_ref, dy_ref, wq_ref, wk_ref, wv_ref, wo_ref, q_ref, k_ref, v_ref, g_ref):
    normed = n_ref[...]
    q_ref[...] = (dot(normed, wq_ref[...]).astype(bf16) * SCALE).astype(bf16)
    k_ref[...] = dot(normed, wk_ref[...]).astype(bf16)
    v_ref[...] = dot(normed, wv_ref[...]).astype(bf16)
    g_ref[...] = dot(dy_ref[...], wo_ref[...], NT).astype(bf16)


def project_call(normed, dy, wq, wk, wv, wo):
    return pl.pallas_call(
        project_kernel,
        out_shape=[jax.ShapeDtypeStruct((CELLS, D), bf16)] * 4,
        compiler_params=params(32),
    )(normed, dy, wq, wk, wv, wo)


def attend_kernel(
    near_ref, count_ref, core_ref, q_ref, k_ref, v_ref, g_ref, n_ref, lo_ref, hi_ref, an_ref, dy_ref,
    wk_ref, wv_ref,
    att_ref, qg_ref, kg_ref, vg_ref, keep_ref, send_ref,
    keys, values, keys_t, values_t, bias, att_t, normed_all,
):
    normed_all[0:CELLS, :] = n_ref[...]
    normed_all[CELLS:CELLS + BS, :] = lo_ref[...]
    normed_all[CELLS + BS:POOL_ROWS, :] = hi_ref[...]
    normed_all[POOL_ROWS:, :] = an_ref[...]
    outside = normed_all[CELLS:, :]
    keys[0:CELLS, :] = k_ref[...]
    values[0:CELLS, :] = v_ref[...]
    keys[CELLS:, :] = dot(outside, wk_ref[...]).astype(bf16)
    values[CELLS:, :] = dot(outside, wv_ref[...]).astype(bf16)
    keys_t[...] = keys[...].T
    values_t[...] = values[...].T

    row = lax.broadcasted_iota(jnp.int32, (BS, BS), 0)
    for block in range(4):
        for j in range(2):
            used = (near_ref[j, 0] == block) | (near_ref[j, 1] == block) | (near_ref[j, 2] == block)
            live = jnp.where(used, BS if block < 2 else count_ref[max(block - 2, 0)], 0)
            bias[block * BS:(block + 1) * BS, j * BS:(j + 1) * BS] = jnp.where(row < live, 0.0, MASKED)

    lane = lax.broadcasted_iota(jnp.int32, (CELLS, PAIR), 1)

    def softmax(scores):
        highest = jnp.max(scores, axis=0, keepdims=True)
        powers = jnp.exp(scores - highest)
        return powers * (1.0 / jnp.sum(powers, axis=0, keepdims=True))

    def score_grad(probs, prob_grad):
        weighted = probs * prob_grad
        return weighted - probs * jnp.sum(weighted, axis=0, keepdims=True)

    def pair_step(pair, carry):
        start = pl.multiple_of(pair * PAIR, PAIR)
        cols = pl.ds(start, PAIR)
        k_pair = keys[:, cols]
        v_pair = values[:, cols]
        q_pair = q_ref[:, cols]
        g_pair = g_ref[:, cols]
        key_term = None
        value_term = None
        out_t = []
        qg_t = []
        for half in range(2):
            mine = (lane >= HEAD) if half else (lane < HEAD)
            q_head = jnp.where(mine, q_pair, jnp.zeros_like(q_pair))
            g_head = jnp.where(mine, g_pair, jnp.zeros_like(g_pair))
            scores = dot(k_pair, q_head, NT)
            prob_grad = dot(v_pair, g_head, NT)
            near = softmax(scores[:POOL_ROWS] + bias[...])
            anchor = softmax(scores[POOL_ROWS:])
            probs = jnp.concatenate([near.astype(bf16), anchor.astype(bf16)], 0)
            grads = jnp.concatenate(
                [
                    score_grad(near, prob_grad[:POOL_ROWS]).astype(bf16),
                    score_grad(anchor, prob_grad[POOL_ROWS:]).astype(bf16),
                ],
                0,
            )
            head_rows = pl.ds(pl.multiple_of(start + half * HEAD, HEAD), HEAD)
            out_t.append(dot(values_t[head_rows, :], probs))
            qg_t.append(dot(keys_t[head_rows, :], grads) * SCALE)
            k_new = dot(grads, q_head)
            v_new = dot(probs, g_head)
            key_term = k_new if key_term is None else key_term + k_new
            value_term = v_new if value_term is None else value_term + v_new
        kg_ref[:, cols] = key_term.astype(bf16)
        vg_ref[:, cols] = value_term.astype(bf16)
        out_pair = jnp.concatenate(out_t, 0).astype(bf16)
        att_t[pl.ds(start, PAIR), :] = out_pair
        att_ref[:, cols] = out_pair.T
        qg_ref[:, cols] = jnp.concatenate(qg_t, 0).astype(bf16).T
        return carry

    lax.fori_loop(0, HEADS // 2, pair_step, 0)

    normed_t = normed_all[...].T
    core = core_ref[0]

    def owner_rows(term):
        parts = [term[48 * m + 24 * low:48 * m + 24 * low + 24] for low in range(2) for m in range(16)]
        return jnp.concatenate(parts, 0).astype(bf16)

    for target, side in ((keep_ref, core), (send_ref, 1 - core)):
        cols = pl.ds(pl.multiple_of(side * SIDE, SIDE), SIDE)
        target[0] = owner_rows(dot(normed_t[:, :CELLS], qg_ref[:, cols]))
        target[1] = owner_rows(dot(normed_t, kg_ref[:, cols]))
        target[2] = owner_rows(dot(normed_t, vg_ref[:, cols]))
        target[3] = owner_rows(dot(att_t[...], dy_ref[:, cols]))


def attend_call(near, count, core, q, k, v, g, normed, lo, hi, anchors, dy, wk, wv):
    smem = pl.BlockSpec(memory_space=pltpu.SMEM)
    vmem = pl.BlockSpec(memory_space=pltpu.VMEM)
    return pl.pallas_call(
        attend_kernel,
        in_specs=[smem] * 3 + [vmem] * 11,
        out_shape=[
            jax.ShapeDtypeStruct((CELLS, D), bf16),
            jax.ShapeDtypeStruct((CELLS, D), bf16),
            jax.ShapeDtypeStruct((KEY_ROWS, D), bf16),
            jax.ShapeDtypeStruct((KEY_ROWS, D), bf16),
            jax.ShapeDtypeStruct((4, D, SIDE), bf16),
            jax.ShapeDtypeStruct((4, D, SIDE), bf16),
        ],
        scratch_shapes=[
            pltpu.VMEM((KEY_ROWS, D), bf16),
            pltpu.VMEM((KEY_ROWS, D), bf16),
            pltpu.VMEM((D, KEY_ROWS), bf16),
            pltpu.VMEM((D, KEY_ROWS), bf16),
            pltpu.VMEM((POOL_ROWS, CELLS), f32),
            pltpu.VMEM((D, CELLS), bf16),
            pltpu.VMEM((KEY_ROWS, D), bf16),
        ],
        compiler_params=params(48),
    )(near, count, core, q, k, v, g, normed, lo, hi, anchors, dy, wk, wv)


def back_kernel(x_ref, att_ref, qg_ref, kg_ref, vg_ref, wq_ref, wk_ref, wv_ref, wo_ref,
                mixed_ref, own_ref, lo_ref, hi_ref, an_ref):
    kv = dot(kg_ref[...], wk_ref[...], NT) + dot(vg_ref[...], wv_ref[...], NT)
    own_ref[...] = kv[:CELLS] + dot(qg_ref[...], wq_ref[...], NT)
    lo_ref[...] = kv[CELLS:CELLS + BS].astype(bf16)
    hi_ref[...] = kv[CELLS + BS:POOL_ROWS].astype(bf16)
    an_ref[...] = kv[POOL_ROWS:].astype(bf16)
    mixed_ref[...] = (x_ref[...].astype(f32) + dot(att_ref[...], wo_ref[...])).astype(bf16)


def back_call(x, att, qg, kg, vg, wq, wk, wv, wo):
    return pl.pallas_call(
        back_kernel,
        out_shape=[
            jax.ShapeDtypeStruct((CELLS, D), bf16),
            jax.ShapeDtypeStruct((CELLS, D), f32),
            jax.ShapeDtypeStruct((BS, D), bf16),
            jax.ShapeDtypeStruct((BS, D), bf16),
            jax.ShapeDtypeStruct((ANCHORS, D), bf16),
        ],
        compiler_params=params(40),
    )(x, att, qg, kg, vg, wq, wk, wv, wo)


def final_kernel(x_ref, dy_ref, own_ref, lo_ref, hi_ref, an_ref, anchor_ref, face_ref, out_ref):
    x = x_ref[...].astype(f32)
    inverse = lax.rsqrt(jnp.mean(x * x, axis=-1, keepdims=True) + EPSILON)

    def placed(index_row, rows):
        cells = lax.broadcasted_iota(jnp.int32, (CELLS, index_row.shape[1]), 0)
        return dot((cells == index_row).astype(bf16), rows)

    normed_grad = (
        own_ref[...]
        + placed(face_ref[0:1, :], lo_ref[...])
        + placed(face_ref[1:2, :], hi_ref[...])
        + placed(anchor_ref[...], an_ref[...])
    )
    cube = inverse * inverse * inverse
    out_ref[...] = (
        dy_ref[...].astype(f32)
        + inverse * normed_grad
        - x * cube * jnp.mean(normed_grad * x, axis=-1, keepdims=True)
    ).astype(bf16)


def final_call(x, dy, own, from_lo, from_hi, from_anchors, anchor_tiled, face_rows):
    return pl.pallas_call(
        final_kernel,
        out_shape=jax.ShapeDtypeStruct((CELLS, D), bf16),
        compiler_params=params(32),
    )(x, dy, own, from_lo, from_hi, from_anchors, anchor_tiled, face_rows)


PLANE = ("y", "xl", "xh")


def swapped(value, axis):
    return lax.ppermute(value, axis, [(0, 1), (1, 0)])


def shifted(value, axis, step):
    count = lax.axis_size(axis)
    return lax.ppermute(value, axis, [(i, (i + step) % count) for i in range(count)])


def along(value, step):
    count = 32
    pairs = [(i, i + step) for i in range(count) if 0 <= i + step < count]
    return lax.ppermute(value, ("z", "xl", "core"), pairs)


def reduced(keep, send):
    arrived = swapped(send, "core")
    both = (keep.astype(f32) + arrived.astype(f32)).astype(bf16)
    spread = lax.all_to_all(both.reshape(16, 192, SIDE), PLANE, 0, 0, tiled=True)
    plane = jnp.sum(spread.astype(f32), axis=0).astype(bf16)
    column = lax.all_to_all(plane.reshape(8, 24, SIDE), "z", 0, 0, tiled=True)
    rows = jnp.sum(column.astype(f32), axis=0).reshape(2, 12, SIDE)
    core = lax.axis_index("core")
    mine = lax.dynamic_index_in_dim(rows, core, 0, keepdims=False)
    other = swapped(lax.dynamic_index_in_dim(rows, 1 - core, 0, keepdims=False), "core")
    return jnp.where(
        core == 0,
        jnp.concatenate([mine, other], 1),
        jnp.concatenate([other, mine], 1),
    )


def body(
    cell_features,
    cotangent,
    query_weight,
    key_weight,
    value_weight,
    out_weight,
    anchor_index,
    face_cells,
    halo_count,
    neighbour_blocks,
):
    x = cell_features[0]
    dy = cotangent[0]
    face_rows = face_cells.reshape(2, BS)
    normed, sent_anchors, sent_lo, sent_hi = send_call(x, anchor_index, face_rows)
    from_lo = along(sent_hi, 1)
    from_hi = along(sent_lo, -1)
    column = jnp.concatenate(
        [sent_anchors] + [shifted(sent_anchors, "y", -k) for k in (1, 2, 3)], 0
    )
    anchors = jnp.concatenate([column, swapped(column, "xh")], 0)
    weights = (query_weight, key_weight, value_weight, out_weight)
    q, k, v, g = project_call(normed, dy, *weights)
    core = lax.axis_index("core").astype(jnp.int32).reshape(1)
    att, qg, kg, vg, keep, send = attend_call(
        neighbour_blocks.reshape(2, NB), halo_count.reshape(2), core, q, k, v, g,
        normed, from_lo, from_hi, anchors, dy, key_weight, value_weight,
    )
    mixed, own, to_lo, to_hi, to_anchors = back_call(x, att, qg, kg, vg, *weights)
    back_hi = along(to_lo, -1)
    back_lo = along(to_hi, 1)
    crossed = swapped(to_anchors[128:], "xh")
    shares = jnp.concatenate(
        [to_anchors[:128].reshape(4, 32, D), crossed.reshape(4, 32, D)], 1
    )
    back_anchors = jnp.concatenate(
        [shares[0]] + [shifted(shares[k], "y", k) for k in (1, 2, 3)], 0
    )
    cell_grad = final_call(
        x, dy, own, back_lo, back_hi, back_anchors, jnp.tile(anchor_index, (1, 8)), face_rows
    )
    weight_grads = reduced(keep, send)
    return mixed[None], cell_grad[None], weight_grads


def solution(mesh):
    fine = Mesh(mesh.devices.reshape(4, 2, 8, 2, 2), ("y", "xh", "z", "xl", "core"))
    dom = ("z", "xl", "core")
    blk = ("y", "xh")
    return jax.shard_map(
        body,
        mesh=fine,
        in_specs=(
            P(dom, blk, None),
            P(dom, blk, None),
            P(),
            P(),
            P(),
            P(),
            P(dom, blk),
            P(dom, blk, None, None),
            P(dom, blk, None),
            P(dom, blk, None),
        ),
        out_specs=(P(dom, blk, None), P(dom, blk, None), P(blk + dom, None)),
        check_vma=False,
    )
```

time: 1600 us -> 130 us (0.08)
  the two profiles are of different devices: /device:TPU:24 before, /device:TPU:36 now
where the time goes in v1:
time: 130 us; the launch traced here: 129 us
  starting transfers between devices  40 us (31%)
  waiting for transfers between devices  36.8 us (28%)
  Pallas kernels  26.4 us (20%)
  local copies, waits for them, and re-layouts  17.6 us (14%)
  other arithmetic  7.07 us (5%)
    all_to_all x1, waiting for transfers between devices, reduced(): lax.all_to_all(both.reshape(16, 192, SIDE), PLANE, 0, 0, tiled=True)  21.6 us
    pallas_call x1, Pallas kernels, attend_call(): pl.pallas_call(attend_kernel, in_specs=[smem] * 3 + [vmem] * 11, out_shap...  19.8 us
    unnamed x70, local copies, waits for them, and re-layouts  17.5 us
    ppermute x4, starting transfers between devices, along(): return lax.ppermute(value, ('z', 'xl', 'core'), pairs)  12.9 us
    ppermute x4, waiting for transfers between devices, swapped(): return lax.ppermute(value, axis, [(0, 1), (1, 0)])  11.4 us
    ppermute x6, starting transfers between devices, shifted(): lax.ppermute(value, axis, [(i, (i + step) % count) for i in range(count)])  9.61 us
    all_to_all x1, starting transfers between devices, reduced(): column = lax.all_to_all(plane.reshape(8, 24, SIDE), 'z', 0, 0, tiled=True)  9.25 us
    all_to_all x1, starting transfers between devices, reduced(): lax.all_to_all(both.reshape(16, 192, SIDE), PLANE, 0, 0, tiled=True)  7.33 us
  transfers between devices with their start and end apart: 16, of which 6 were waited for; matrix products, arithmetic and copies ran while one was open for 2% of the time, Pallas kernels for 5%

profile of v1, /device:TPU:36, one launch (start us, length us, event | category | flops | bytes accessed | tf_op | source)
XLA Modules:
  0.0 129.0 jit_solution(2894943778026606440)
XLA Ops:
  3.4 3.1 %collective-permute-start.2 = (bf16[32,768]{1,0:T(8,128)(2,1)S(1)}, bf16[32,768]{1,0:T(8,128)(2,1)S(1)}, u32[]{:S(2)}, u32[]{:S(2)}) collective-permute-start(bf16[32,768]{1,0:T(8,128)(2,1)S(1)} %get-tuple-element.29), channel_id=1, source_target_pairs={{0,192},{64,0},{128,64},{192,128},{1,193},{65,1},{129,65},{193,129... | collective-permute-start | bytes 147464 | tf_op jit(solution)/shard_map/ppermute | solution.py:265
  8.1 1.9 %collective-permute-start = (bf16[128,768]{1,0:T(8,128)(2,1)S(1)}, bf16[128,768]{1,0:T(8,128)(2,1)S(1)}, u32[]{:S(2)}, u32[]{:S(2)}) collective-permute-start(bf16[128,768]{1,0:T(8,128)(2,1)S(1)} %get-tuple-element.27), channel_id=1, source_target_pairs={{0,1},{1,2},{2,3},{3,4},{4,5},{5,6},{6,7},{7,8},{8,9},{9,10},{10,1... | collective-permute-start | bytes 589832 | tf_op jit(solution)/shard_map/ppermute | solution.py:271
  10.0 4.5 %collective-permute-start.1 = (bf16[128,768]{1,0:T(8,128)(2,1)S(1)}, bf16[128,768]{1,0:T(8,128)(2,1)S(1)}, u32[]{:S(2)}, u32[]{:S(2)}) collective-permute-start(bf16[128,768]{1,0:T(8,128)(2,1)S(1)} %get-tuple-element.28), channel_id=1, source_target_pairs={{1,0},{2,1},{3,2},{4,3},{5,4},{6,5},{7,6},{8,7},{9,8},{10,9},{11,1... | collective-permute-start | bytes 589832 | tf_op jit(solution)/shard_map/ppermute | solution.py:271
  15.9 1.3 copy-done.2
  17.2 1.3 copy-done.4
  18.4 1.3 copy-done.6
  20.7 1.4 %shard_map.122 = (bf16[256,768]{1,0:T(8,128)(2,1)S(1)}, bf16[256,768]{1,0:T(8,128)(2,1)S(1)}, bf16[256,768]{1,0:T(8,128)(2,1)S(1)}, bf16[256,768]{1,0:T(8,128)(2,1)S(1)}) custom-call(bf16[256,768]{1,0:T(8,128)(2,1)S(1)} %get-tuple-element.22.n_ref, bf16[256,768]{1,0:T(8,128)(2,1)S(1)} %bitcast.28, bf16[768,768]{1,0:T(8,128)(2,1)S(1)} %copy-done.4, ...), custom_call_target="tpu_custom_call" | custom-call | tf_op jit(solution)/shard_map/pallas_call | solution.py:73
  22.8 6.6 %collective-permute-done.5 = bf16[128,768]{1,0:T(8,128)(2,1)S(1)} collective-permute-done((bf16[128,768]{1,0:T(8,128)(2,1)S(1)}, bf16[128,768]{1,0:T(8,128)(2,1)S(1)}, u32[]{:S(2)}, u32[]{:S(2)}) %collective-permute-start.5) | collective-permute-done | bytes 196640 | tf_op jit(solution)/shard_map/ppermute | solution.py:260
  29.5 19.8 %shard_map.123 = (bf16[256,768]{1,0:T(8,128)(2,1)S(1)}, bf16[256,768]{1,0:T(8,128)(2,1)S(1)}, bf16[768,768]{1,0:T(8,128)(2,1)S(1)}, bf16[768,768]{1,0:T(8,128)(2...) custom-call(s32[2,3]{1,0:T(2,128)S(1)} %bitcast.34, s32[2]{0:T(128)S(1)} %bitcast.35, s32[1]{0:T(128)} %bitcast.3.core_ref, ...), custom_call_target="tpu_custom_call" | custom-call | tf_op jit(solution)/shard_map/pallas_call | solution.py:178
  49.4 4.7 %collective-permute-done.12 = bf16[4,768,384]{2,1,0:T(8,128)(2,1)S(1)} collective-permute-done((bf16[4,768,384]{2,1,0:T(8,128)(2,1)}, bf16[4,768,384]{2,1,0:T(8,128)(2,1)S(1)}, u32[]{:S(2)}, u32[]{:S(2)}) %collective-permute-start.12) | collective-permute-done | bytes 2359328 | tf_op jit(solution)/shard_map/ppermute | solution.py:260
  54.2 3.7 %add_convert_fusion = bf16[4,768,384]{2,1,0:T(8,128)(2,1)} fusion(bf16[4,768,384]{2,1,0:T(8,128)(2,1)S(1)} %collective-permute-done.12, bf16[4,768,384]{2,1,0:T(8,128)(2,1)} %get-tuple-element.39), kind=kLoop, calls=%fused_computation | loop fusion | flops 4718592 | bytes 7077888 | tf_op jit(solution)/shard_map/convert_element_type | solution.py:276
  57.9 7.3 %all-to-all-start = ((bf16[16,192,384]{2,1,0:T(8,128)(2,1)}), bf16[16,192,384]{2,1,0:T(8,128)(2,1)}, u32[]{:S(2)}, u32[]{:S(2)}) async-start(bf16[16,192,384]{2,1,0:T(8,128)(2,1)} %bitcast.36), calls=%async_computation | async-start | bytes 4718592 | tf_op jit(solution)/shard_map/all_to_all | solution.py:277
  67.5 1.3 copy-done.15
  72.0 3.4 %shard_map.124 = (bf16[256,768]{1,0:T(8,128)(2,1)}, f32[256,768]{1,0:T(8,128)S(1)}, bf16[128,768]{1,0:T(8,128)(2,1)S(1)}, bf16[128,768]{1,0:T(8,128)(2,1)S(1)}, bf16[256,768]{1,0:T(8,128)(2,1)S(1)}) custom-call(bf16[256,768]{1,0:T(8,128)(2,1)S(1)} %bitcast.26, bf16[256,768]{1,0:T(8,128)(2,1)S(1)} %copy-done.20, bf16[256,768]{1,0:T(8,128)(2,1)S(1)} %copy-done.22, ...), custom_call_target="tpu_custom_call" | custom-call | tf_op jit(solution)/shard_map/pallas_call | solution.py:213
  78.0 21.6 %all-to-all-done = bf16[16,192,384]{2,1,0:T(8,128)(2,1)} async-done(((bf16[16,192,384]{2,1,0:T(8,128)(2,1)}), bf16[16,192,384]{2,1,0:T(8,128)(2,1)}, u32[]{:S(2)}, u32[]{:S(2)}) %all-to-all-start) | async-done | bytes 2359328 | tf_op jit(solution)/shard_map/all_to_all | solution.py:277
  99.6 2.7 %reduce_sum.21 = bf16[192,384]{1,0:T(8,128)(2,1)} reduce(bf16[16,192,384]{2,1,0:T(8,128)(2,1)} %all-to-all-done, bf16[]{:T(256)} %constant.16.clone.1), dimensions={0}, to_apply=%region_0.0 | reduce | flops 1105920 | bytes 2506754 | tf_op jit(solution)/shard_map/reduce_sum | solution.py:278
  102.2 9.3 %all-to-all-start.1 = ((bf16[8,24,384]{2,1,0:T(8,128)(2,1)}), bf16[8,24,384]{2,1,0:T(8,128)(2,1)S(1)}, u32[]{:S(2)}, u32[]{:S(2)}) async-start(bf16[8,24,384]{2,1,0:T(8,128)(2,1)} %bitcast.16), calls=%async_computation.1 | async-start | bytes 294912 | tf_op jit(solution)/shard_map/all_to_all | solution.py:279
  111.6 1.9 %collective-permute-start.6 = (bf16[128,768]{1,0:T(8,128)(2,1)S(1)}, bf16[128,768]{1,0:T(8,128)(2,1)S(1)}, u32[]{:S(2)}, u32[]{:S(2)}) collective-permute-start(bf16[128,768]{1,0:T(8,128)(2,1)S(1)} %copy-done.32), channel_id=1, source_target_pairs={{0,1},{1,2},{2,3},{3,4},{4,5},{5,6},{6,7},{7,8},{8,9},{9,10},{10,1... | collective-permute-start | bytes 589832 | tf_op jit(solution)/shard_map/ppermute | solution.py:271
  113.5 4.5 %collective-permute-start.7 = (bf16[128,768]{1,0:T(8,128)(2,1)S(1)}, bf16[128,768]{1,0:T(8,128)(2,1)S(1)}, u32[]{:S(2)}, u32[]{:S(2)}) collective-permute-start(bf16[128,768]{1,0:T(8,128)(2,1)S(1)} %copy-done.30), channel_id=1, source_target_pairs={{1,0},{2,1},{3,2},{4,3},{5,4},{6,5},{7,6},{8,7},{9,8},{10,9},{11,1... | collective-permute-start | bytes 589832 | tf_op jit(solution)/shard_map/ppermute | solution.py:271
  118.1 2.9 %collective-permute-start.10 = (bf16[64,768]{1,0:T(8,128)(2,1)S(1)}, bf16[64,768]{1,0:T(8,128)(2,1)S(1)}, u32[]{:S(2)}, u32[]{:S(2)}) collective-permute-start(bf16[64,768]{1,0:T(8,128)(2,1)S(1)} %get-tuple-element.44), channel_id=1, source_target_pairs={{0,128},{64,192},{128,0},{192,64},{1,129},{65,193},{129,1},{193,65... | collective-permute-start | bytes 294920 | tf_op jit(solution)/shard_map/ppermute | solution.py:265
  121.1 1.9 %collective-permute-start.9 = (bf16[64,768]{1,0:T(8,128)(2,1)S(1)}, bf16[64,768]{1,0:T(8,128)(2,1)S(1)}, u32[]{:S(2)}, u32[]{:S(2)}) collective-permute-start(bf16[64,768]{1,0:T(8,128)(2,1)S(1)} %get-tuple-element.42), channel_id=1, source_target_pairs={{0,64},{64,128},{128,192},{192,0},{1,65},{65,129},{129,193},{193,1... | collective-permute-start | bytes 294920 | tf_op jit(solution)/shard_map/ppermute | solution.py:265
  123.1 1.3 %collective-permute-done.10 = bf16[64,768]{1,0:T(8,128)(2,1)S(1)} collective-permute-done((bf16[64,768]{1,0:T(8,128)(2,1)S(1)}, bf16[64,768]{1,0:T(8,128)(2,1)S(1)}, u32[]{:S(2)}, u32[]{:S(2)}) %collective-permute-start.10) | collective-permute-done | bytes 98336 | tf_op jit(solution)/shard_map/ppermute | solution.py:265
  125.6 1.3 %collective-permute-done.9 = bf16[64,768]{1,0:T(8,128)(2,1)S(1)} collective-permute-done((bf16[64,768]{1,0:T(8,128)(2,1)S(1)}, bf16[64,768]{1,0:T(8,128)(2,1)S(1)}, u32[]{:S(2)}, u32[]{:S(2)}) %collective-permute-start.9) | collective-permute-done | bytes 98336 | tf_op jit(solution)/shard_map/ppermute | solution.py:265
  127.0 1.4 %shard_map.125 = bf16[256,768]{1,0:T(8,128)(2,1)} custom-call(bf16[256,768]{1,0:T(8,128)(2,1)S(1)} %bitcast.27, bf16[256,768]{1,0:T(8,128)(2,1)S(1)} %bitcast.30, f32[256,768]{1,0:T(8,128)S(1)} %copy-done.18, bf16[128,768]{1,0:T(8,128)(2,1)S(1)} %collective-permute-done.6.lo_ref, bf16[128,768]{1,0:T(8,128)(2,1)S(1)} %collective-permute-done.7.hi_ref, ...), custom_call_target="tpu_custom_call" | custom-call | tf_op jit(solution)/shard_map/pallas_call | solution.py:249
  (96 shorter events, 17.6 us)
Async XLA Ops:
  3.4 18.7 %collective-permute-start.2 = (bf16[32,768]{1,0:T(8,128)(2,1)S(1)}, bf16[32,768]{1,0:T(8,128)(2,1)S(1)}, u32[]{:S(2)}, u32[]{:S(2)}) collective-permute-start(bf16[32,768]{1,0:T(8,128)(2,1)S(1)} %get-tuple-element.29), channel_id=1, source_target_pairs={{0,192},{64,0},{128,64},{192,128},{1,193},{65,1},{129,65},{193,129... | collective-permute-start | bytes 147464 | tf_op jit(solution)/shard_map/ppermute | solution.py:265
  6.5 15.6 %collective-permute-start.3 = (bf16[32,768]{1,0:T(8,128)(2,1)S(1)}, bf16[32,768]{1,0:T(8,128)(2,1)S(1)}, u32[]{:S(2)}, u32[]{:S(2)}) collective-permute-start(bf16[32,768]{1,0:T(8,128)(2,1)S(1)} %get-tuple-element.29), channel_id=1, source_target_pairs={{0,128},{64,192},{128,0},{192,64},{1,129},{65,193},{129,1},{193,65... | collective-permute-start | bytes 147464 | tf_op jit(solution)/shard_map/ppermute | solution.py:265
  7.1 15.0 %collective-permute-start.4 = (bf16[32,768]{1,0:T(8,128)(2,1)S(1)}, bf16[32,768]{1,0:T(8,128)(2,1)S(1)}, u32[]{:S(2)}, u32[]{:S(2)}) collective-permute-start(bf16[32,768]{1,0:T(8,128)(2,1)S(1)} %get-tuple-element.29), channel_id=1, source_target_pairs={{0,64},{64,128},{128,192},{192,0},{1,65},{65,129},{129,193},{193,1... | collective-permute-start | bytes 147464 | tf_op jit(solution)/shard_map/ppermute | solution.py:265
  8.1 21.3 %collective-permute-start = (bf16[128,768]{1,0:T(8,128)(2,1)S(1)}, bf16[128,768]{1,0:T(8,128)(2,1)S(1)}, u32[]{:S(2)}, u32[]{:S(2)}) collective-permute-start(bf16[128,768]{1,0:T(8,128)(2,1)S(1)} %get-tuple-element.27), channel_id=1, source_target_pairs={{0,1},{1,2},{2,3},{3,4},{4,5},{5,6},{6,7},{7,8},{8,9},{9,10},{10,1... | collective-permute-start | bytes 589832 | tf_op jit(solution)/shard_map/ppermute | solution.py:271
  10.0 19.4 %collective-permute-start.1 = (bf16[128,768]{1,0:T(8,128)(2,1)S(1)}, bf16[128,768]{1,0:T(8,128)(2,1)S(1)}, u32[]{:S(2)}, u32[]{:S(2)}) collective-permute-start(bf16[128,768]{1,0:T(8,128)(2,1)S(1)} %get-tuple-element.28), channel_id=1, source_target_pairs={{1,0},{2,1},{3,2},{4,3},{5,4},{6,5},{7,6},{8,7},{9,8},{10,9},{11,1... | collective-permute-start | bytes 589832 | tf_op jit(solution)/shard_map/ppermute | solution.py:271
  20.7 8.8 %copy-start.28 = (s32[1,1,2]{2,1,0:T(1,128)S(1)}, s32[1,1,2]{2,1,0:T(1,128)}, u32[]{:S(2)}) copy-start(s32[1,1,2]{2,1,0:T(1,128)} %param.18) | copy-start | bytes 28
  22.1 7.3 %collective-permute-start.5 = (bf16[128,768]{1,0:T(8,128)(2,1)S(1)}, bf16[128,768]{1,0:T(8,128)(2,1)S(1)}, u32[]{:S(2)}, u32[]{:S(2)}) collective-permute-start(bf16[128,768]{1,0:T(8,128)(2,1)S(1)} %pad_maximum_fusion.1), channel_id=1, source_target_pairs={{0,32},{32,0},{1,33},{33,1},{2,34},{34,2},{3,35},{35,3},{4,36},{36... | collective-permute-start | bytes 589832 | tf_op jit(solution)/shard_map/ppermute | solution.py:260
  49.3 4.8 %collective-permute-start.12 = (bf16[4,768,384]{2,1,0:T(8,128)(2,1)}, bf16[4,768,384]{2,1,0:T(8,128)(2,1)S(1)}, u32[]{:S(2)}, u32[]{:S(2)}) collective-permute-start(bf16[4,768,384]{2,1,0:T(8,128)(2,1)} %get-tuple-element.40), channel_id=1, source_target_pairs={{0,1},{1,0},{2,3},{3,2},{4,5},{5,4},{6,7},{7,6},{8,9},{9,8},{10,11... | collective-permute-start | bytes 7077896 | tf_op jit(solution)/shard_map/ppermute | solution.py:260
  57.9 41.7 %all-to-all-start = ((bf16[16,192,384]{2,1,0:T(8,128)(2,1)}), bf16[16,192,384]{2,1,0:T(8,128)(2,1)}, u32[]{:S(2)}, u32[]{:S(2)}) async-start(bf16[16,192,384]{2,1,0:T(8,128)(2,1)} %bitcast.36), calls=%async_computation | async-start | bytes 4718592 | tf_op jit(solution)/shard_map/all_to_all | solution.py:277
  76.8 34.7 %copy-start.26 = (s32[1,32]{1,0:T(1,128)S(1)}, s32[1,32]{1,0:T(1,128)}, u32[]{:S(2)}) copy-start(s32[1,32]{1,0:T(1,128)} %anchor_ref.1) | copy-start | bytes 388
  76.8 34.8 %copy-start.32 = (bf16[128,768]{1,0:T(8,128)(2,1)S(1)}, bf16[128,768]{1,0:T(8,128)(2,1)}, u32[]{:S(2)}) copy-start(bf16[128,768]{1,0:T(8,128)(2,1)} %copy-done.31) | copy-start | bytes 589828
  76.8 36.7 %copy-start.30 = (bf16[128,768]{1,0:T(8,128)(2,1)S(1)}, bf16[128,768]{1,0:T(8,128)(2,1)}, u32[]{:S(2)}) copy-start(bf16[128,768]{1,0:T(8,128)(2,1)} %copy-done.29) | copy-start | bytes 589828
  77.7 49.3 %copy-start.10 = (bf16[1,256,768]{2,1,0:T(8,128)(2,1)S(1)}, bf16[1,256,768]{2,1,0:T(8,128)(2,1)}, u32[]{:S(2)}) copy-start(bf16[1,256,768]{2,1,0:T(8,128)(2,1)} %param.10) | copy-start | bytes 1179652
  77.7 49.3 %copy-start.13 = (bf16[1,256,768]{2,1,0:T(8,128)(2,1)S(1)}, bf16[1,256,768]{2,1,0:T(8,128)(2,1)}, u32[]{:S(2)}) copy-start(bf16[1,256,768]{2,1,0:T(8,128)(2,1)} %param.11) | copy-start | bytes 1179652
  77.7 49.3 %copy-start.18 = (f32[256,768]{1,0:T(8,128)S(1)}, f32[256,768]{1,0:T(8,128)}, u32[]{:S(2)}) copy-start(f32[256,768]{1,0:T(8,128)} %copy-done.17) | copy-start | bytes 2359300
  77.7 49.3 %copy-start.24 = (s32[1,1,2,128]{3,2,1,0:T(2,128)S(1)}, s32[1,1,2,128]{3,2,1,0:T(2,128)}, u32[]{:S(2)}) copy-start(s32[1,1,2,128]{3,2,1,0:T(2,128)} %param.17) | copy-start | bytes 3076
  77.7 40.3 %collective-permute-start.8 = (bf16[128,768]{1,0:T(8,128)(2,1)S(1)}, bf16[128,768]{1,0:T(8,128)(2,1)S(1)}, u32[]{:S(2)}, u32[]{:S(2)}) collective-permute-start(bf16[128,768]{1,0:T(8,128)(2,1)S(1)} %get-tuple-element.46), channel_id=1, source_target_pairs={{0,32},{32,0},{1,33},{33,1},{2,34},{34,2},{3,35},{35,3},{4,36},{36... | collective-permute-start | bytes 589832 | tf_op jit(solution)/shard_map/ppermute | solution.py:260
  102.2 20.8 %all-to-all-start.1 = ((bf16[8,24,384]{2,1,0:T(8,128)(2,1)}), bf16[8,24,384]{2,1,0:T(8,128)(2,1)S(1)}, u32[]{:S(2)}, u32[]{:S(2)}) async-start(bf16[8,24,384]{2,1,0:T(8,128)(2,1)} %bitcast.16), calls=%async_computation.1 | async-start | bytes 294912 | tf_op jit(solution)/shard_map/all_to_all | solution.py:279
  111.6 15.4 %collective-permute-start.6 = (bf16[128,768]{1,0:T(8,128)(2,1)S(1)}, bf16[128,768]{1,0:T(8,128)(2,1)S(1)}, u32[]{:S(2)}, u32[]{:S(2)}) collective-permute-start(bf16[128,768]{1,0:T(8,128)(2,1)S(1)} %copy-done.32), channel_id=1, source_target_pairs={{0,1},{1,2},{2,3},{3,4},{4,5},{5,6},{6,7},{7,8},{8,9},{9,10},{10,1... | collective-permute-start | bytes 589832 | tf_op jit(solution)/shard_map/ppermute | solution.py:271
  113.5 13.4 %collective-permute-start.7 = (bf16[128,768]{1,0:T(8,128)(2,1)S(1)}, bf16[128,768]{1,0:T(8,128)(2,1)S(1)}, u32[]{:S(2)}, u32[]{:S(2)}) collective-permute-start(bf16[128,768]{1,0:T(8,128)(2,1)S(1)} %copy-done.30), channel_id=1, source_target_pairs={{1,0},{2,1},{3,2},{4,3},{5,4},{6,5},{7,6},{8,7},{9,8},{10,9},{11,1... | collective-permute-start | bytes 589832 | tf_op jit(solution)/shard_map/ppermute | solution.py:271
  118.1 6.3 %collective-permute-start.10 = (bf16[64,768]{1,0:T(8,128)(2,1)S(1)}, bf16[64,768]{1,0:T(8,128)(2,1)S(1)}, u32[]{:S(2)}, u32[]{:S(2)}) collective-permute-start(bf16[64,768]{1,0:T(8,128)(2,1)S(1)} %get-tuple-element.44), channel_id=1, source_target_pairs={{0,128},{64,192},{128,0},{192,64},{1,129},{65,193},{129,1},{193,65... | collective-permute-start | bytes 294920 | tf_op jit(solution)/shard_map/ppermute | solution.py:265
  121.0 4.6 %collective-permute-start.11 = (bf16[64,768]{1,0:T(8,128)(2,1)S(1)}, bf16[64,768]{1,0:T(8,128)(2,1)S(1)}, u32[]{:S(2)}, u32[]{:S(2)}) collective-permute-start(bf16[64,768]{1,0:T(8,128)(2,1)S(1)} %get-tuple-element.43), channel_id=1, source_target_pairs={{0,192},{64,0},{128,64},{192,128},{1,193},{65,1},{129,65},{193,129... | collective-permute-start | bytes 294920 | tf_op jit(solution)/shard_map/ppermute | solution.py:265
  121.1 5.8 %collective-permute-start.9 = (bf16[64,768]{1,0:T(8,128)(2,1)S(1)}, bf16[64,768]{1,0:T(8,128)(2,1)S(1)}, u32[]{:S(2)}, u32[]{:S(2)}) collective-permute-start(bf16[64,768]{1,0:T(8,128)(2,1)S(1)} %get-tuple-element.42), channel_id=1, source_target_pairs={{0,64},{64,128},{128,192},{192,0},{1,65},{65,129},{129,193},{193,1... | collective-permute-start | bytes 294920 | tf_op jit(solution)/shard_map/ppermute | solution.py:265
  124.4 4.0 %collective-permute-start.13 = (f32[12,384]{1,0:T(8,128)S(1)}, f32[12,384]{1,0:T(8,128)S(1)}, u32[]{:S(2)}, u32[]{:S(2)}) collective-permute-start(f32[12,384]{1,0:T(8,128)S(1)} %get-tuple-element.48), channel_id=1, source_target_pairs={{0,1},{1,0},{2,3},{3,2},{4,5},{5,4},{6,7},{7,6},{8,9},{9,8},{10,11... | collective-permute-start | bytes 55304 | tf_op jit(solution)/shard_map/ppermute | solution.py:260
  (25 other events, 82.6 us)
